TPU v7x, 32 devices: a whole 2x2x4 slice. The times are simulated.
32 devices in a mesh: dp: 2 (over x), section: 4 (over z), tm: 4 (over y, core).
Axes of the slice: x: 2, y: 2, z: 4, core: 2. Of those that a mesh axis runs over, the one named last changes fastest.
Arguments:
- frames: bfloat16 [4, 512, 1280], P('dp', 'tm'), may hold values from -6 to 6
- block_mask: int32 [4, 8, 2], P('dp', 'tm'), may hold values 0 or 1
- span_segment: int32 [4, 8], P('dp'), may hold values from 0 to 3, as said below
- dec_states: bfloat16 [512, 1280], P(('dp', 'tm')), may hold values from -6 to 6
- enc_qkv: bfloat16 [4, 1280, 1920], P('section', ('dp', 'tm')), may hold values from -0.15625 to 0.15625
- enc_out: bfloat16 [4, 640, 1280], P('section', None, ('dp', 'tm')), may hold values from -0.75 to 0.75
- cross_query: bfloat16 [1280, 768], P(('dp', 'tm'), 'section'), may hold values from -0.15625 to 0.15625
- cross_key: bfloat16 [1280, 768], P(('dp', 'tm'), 'section'), may hold values from -0.15625 to 0.15625
- cross_value: bfloat16 [1280, 768], P(('dp', 'tm'), 'section'), may hold values from -0.75 to 0.75
- cotangent: bfloat16 [512, 1280], P(('dp', 'tm')), may hold values from -1.5 to 1.5
Outputs:
- context: bfloat16 [512, 768], P(('dp', 'tm'), 'section')
- out_grad: float32 [768, 1280], P('section', ('dp', 'tm'))
Inputs may be any that keep to these rules, and one draw needn't show every extreme that they name: `span_segment`: the first of every 2 blocks, block d * 2, serves segment (d + 2) mod 4; every other block serves a segment drawn evenly.
All inputs are finite; a program needn't handle non-finite values. No bound on the sum of `block_mask` on one device may be relied on, other than what follows from the above.
Results may differ from a plain program's by a relative error of at most 0.011.
Values may be sent and summed in bfloat16 or wider, within the bound.
A program may use at most 64 MiB of HBM per device.

v0:
```python
import functools

import jax
import jax.numpy as jnp
from jax import lax
from jax.experimental import pallas as pl
from jax.experimental.pallas import tpu as pltpu
from jax.sharding import PartitionSpec as P

HD = 64
BLK = 64
MB = 2

MESH = pl.DeviceIdType.MESH
epsilon = 1e-05
SCALE = HD ** (-0.5)


def norm_rows(inputs):
    values32 = inputs.astype(jnp.float32)
    center = values32 - jnp.mean(values32, axis=-1, keepdims=True)
    spread = jnp.mean(center * center, axis=-1, keepdims=True)
    return (center * lax.rsqrt(spread + epsilon)).astype(jnp.bfloat16)


def dot_nt(a, b):
    return lax.dot_general(a, b, (((1,), (1,)), ((), ())), preferred_element_type=jnp.float32)


def dot_nn(a, b):
    return jnp.dot(a, b, preferred_element_type=jnp.float32)


def kernel(
    sizes,
    frames,
    enc_mask,
    cross_mask,
    dec,
    cot,
    qkv,
    out_w,
    query_w,
    both_w,
    context_out,
    grad_out,
    xbuf,
    ybuf,
    kvbuf,
    memn,
    qall,
    part,
    part_in,
    ctx_all,
    cot_all,
    x_send,
    x_recv,
    halo_send,
    halo_recv,
    mem_send,
    mem_recv,
    q_send,
    q_recv,
    part_send,
    part_recv,
    ctx_send,
    ctx_recv,
    cot_send,
    cot_recv,
):
    n_dp, n_sec, n_tm = sizes
    group = n_dp * n_tm
    dp, sec, tm = (lax.axis_index(a) for a in ("dp", "section", "tm"))
    me = dp * n_tm + tm
    rows = frames.shape[1]
    width = out_w.shape[0]
    heads = width // HD
    cross_width = query_w.shape[1]
    cross_heads = cross_width // HD
    chunks = rows // BLK
    tokens = qall.shape[2]
    first, last = sec == 0, sec == n_sec - 1

    def peer(d):
        other = lax.rem(me + d, group)
        return other, {"dp": other // n_tm, "tm": lax.rem(other, n_tm)}

    def remote(src, dst, send, recv, where):
        return pltpu.make_async_remote_copy(
            src_ref=src, dst_ref=dst, send_sem=send, recv_sem=recv, device_id=where, device_id_type=MESH
        )

    def each(count, body, start=0):
        lax.fori_loop(start, count, lambda i, c: (body(i), c)[1], 0)

    def x_copy(m):
        return remote(ybuf.at[m], xbuf.at[m], x_send.at[m], x_recv.at[m], {"section": sec + 1})

    def halo_up(m):
        return remote(
            kvbuf.at[m, pl.ds(rows, BLK)], kvbuf.at[m, pl.ds(0, BLK)],
            halo_send.at[0, m], halo_recv.at[0, m], {"tm": tm + 1},
        )

    def halo_down(m):
        return remote(
            kvbuf.at[m, pl.ds(BLK, BLK)], kvbuf.at[m, pl.ds(rows + BLK, BLK)],
            halo_send.at[1, m], halo_recv.at[1, m], {"tm": tm - 1},
        )

    def mem_copy(m, c):
        return remote(
            memn.at[m, pl.ds(c * BLK, BLK)], memn.at[m, pl.ds(c * BLK, BLK)],
            mem_send.at[m, c], mem_recv.at[m, c], {"section": sec - 1},
        )

    def q_copy(d, slot, sem):
        return remote(
            qall.at[tm], qall.at[slot], q_send.at[d], q_recv.at[sem], {"tm": lax.rem(tm + d, n_tm)}
        )

    def part_copy(m, d, slot):
        to = lax.rem(tm + d, n_tm)
        return remote(
            part.at[m, to], part_in.at[slot, m], part_send.at[m, d], part_recv.at[m, slot], {"tm": to}
        )

    def ctx_copy(d, slot):
        _, where = peer(d)
        return remote(ctx_all.at[me], ctx_all.at[slot], ctx_send.at[d], ctx_recv.at[slot], where)

    def cot_copy(d, slot):
        other, where = peer(d)
        return remote(cot.at[other], cot_all.at[slot], cot_send.at[d], cot_recv.at[slot], where)

    for m in range(MB):
        kvbuf[m, 0:BLK, :] = jnp.zeros((BLK, 2 * width), jnp.bfloat16)
        kvbuf[m, rows + BLK :, :] = jnp.zeros((BLK, 2 * width), jnp.bfloat16)

    barrier = pltpu.get_barrier_semaphore()

    def greet(d):
        _, where = peer(d)
        pl.semaphore_signal(barrier, inc=1, device_id=where, device_id_type=MESH)

    each(group, greet, 1)

    @pl.when(sec > 0)
    def _():
        pl.semaphore_signal(barrier, inc=1, device_id={"section": sec - 1}, device_id_type=MESH)

    @pl.when(sec < n_sec - 1)
    def _():
        pl.semaphore_signal(barrier, inc=1, device_id={"section": sec + 1}, device_id_type=MESH)

    near = jnp.where(sec > 0, 1, 0) + jnp.where(sec < n_sec - 1, 1, 0)
    pl.semaphore_wait(barrier, group - 1 + near)

    each(group, lambda d: cot_copy(d, me).start(), 1)
    cot_all[me] = cot[me]

    def queries():
        values = dot_nn(norm_rows(dec[...]), query_w[...]).astype(jnp.bfloat16)
        qall[tm] = values.reshape(MB, tokens, cross_width)
        each(n_tm, lambda d: q_copy(d, tm, tm).start(), 1)

    @pl.when(sec > 0)
    def _():
        queries()

    def encode(m):
        @pl.when(first)
        def _():
            xbuf[m] = frames[m]

        @pl.when(sec > 0)
        def _():
            x_copy(m).wait_recv()

        normed = norm_rows(xbuf[m])
        kvbuf[m, BLK : BLK + rows, :] = dot_nn(normed, qkv[:, width:]).astype(jnp.bfloat16)

        @pl.when(tm < n_tm - 1)
        def _():
            halo_up(m).start()

        @pl.when(tm > 0)
        def _():
            halo_down(m).start()

        query = dot_nn(normed, qkv[:, :width]).astype(jnp.bfloat16)

        @pl.when(tm > 0)
        def _():
            halo_up(m).wait_recv()

        @pl.when(tm < n_tm - 1)
        def _():
            halo_down(m).wait_recv()

        seen = enc_mask[m] > 0
        parts = []
        for h in range(heads):
            cols = slice(h * HD, (h + 1) * HD)
            scores = dot_nt(query[:, cols], kvbuf[m, :, cols]) * SCALE
            weights = jnp.where(seen, jnp.exp(scores), 0.0)
            totals = jnp.sum(weights, axis=-1, keepdims=True)
            value = kvbuf[m, :, width + h * HD : width + (h + 1) * HD]
            parts.append((dot_nn(weights.astype(jnp.bfloat16), value) / totals).astype(jnp.bfloat16))
        attended = jnp.concatenate(parts, axis=1)
        update = dot_nn(attended, out_w[...])
        finished = (xbuf[m].astype(jnp.float32) + update).astype(jnp.bfloat16)

        @pl.when(sec < n_sec - 1)
        def _():
            ybuf[m] = finished
            x_copy(m).start()

        @pl.when(last)
        def _():
            memn[m] = norm_rows(finished)
            if n_sec > 1:
                for c in range(chunks):
                    mem_copy(m, c).start()

    each(MB, encode)

    @pl.when(first)
    def _():
        queries()

    def q_arrives(d):
        source = lax.rem(tm + n_tm - d, n_tm)
        q_copy(d, source, source).wait_recv()

    each(n_tm, q_arrives, 1)

    def cross(m):
        for c in range(chunks):
            @pl.when(sec < n_sec - 1)
            def _():
                mem_copy(m, c).wait_recv()

            @pl.when((sec < n_sec - 1) & (sec > 0))
            def _():
                mem_copy(m, c).start()

        key_value = dot_nn(memn[m], both_w[...]).astype(jnp.bfloat16)
        query = qall[:, m].reshape(n_tm * tokens, cross_width)
        seen = cross_mask[m] > 0
        sums, denominators = [], []
        for h in range(cross_heads):
            cols = slice(h * HD, (h + 1) * HD)
            scores = dot_nt(query[:, cols], key_value[:, cols]) * SCALE
            weights = jnp.where(seen, jnp.exp(scores), 0.0)
            denominators.append(
                jnp.broadcast_to(jnp.sum(weights, axis=-1, keepdims=True), (n_tm * tokens, HD))
            )
            value = key_value[:, cross_width + h * HD : cross_width + (h + 1) * HD]
            sums.append(dot_nn(weights.astype(jnp.bfloat16), value))
        both = jnp.concatenate(sums + denominators, axis=1)
        part[m] = both.reshape(n_tm, tokens, 2 * cross_width)
        each(n_tm, lambda d: part_copy(m, d, tm).start(), 1)

    each(MB, cross)

    for m in range(MB):
        total = part[m, tm]
        for d in range(1, n_tm):
            source = lax.rem(tm + n_tm - d, n_tm)
            part_copy(m, d, source).wait_recv()
            total = total + part_in[source, m]
        context = (total[:, :cross_width] / total[:, cross_width:]).astype(jnp.bfloat16)
        ctx_all[me, m * tokens : (m + 1) * tokens, :] = context
        context_out[m * tokens : (m + 1) * tokens, :] = context

    each(group, lambda d: ctx_copy(d, me).start(), 1)

    def arrivals(d):
        source = lax.rem(me + group - d, group)
        cot_copy(d, source).wait_recv()
        ctx_copy(d, source).wait_recv()

    each(group, arrivals, 1)
    left = ctx_all[...].reshape(group * MB * tokens, cross_width)
    right = cot_all[...].reshape(group * MB * tokens, cot.shape[2])
    grad_out[...] = lax.dot_general(
        left, right, (((0,), (0,)), ((), ())), preferred_element_type=jnp.float32
    )

    for m in range(MB):
        @pl.when(sec < n_sec - 1)
        def _():
            x_copy(m).wait_send()

        @pl.when(tm < n_tm - 1)
        def _():
            halo_up(m).wait_send()

        @pl.when(tm > 0)
        def _():
            halo_down(m).wait_send()

        @pl.when(sec > 0)
        def _():
            for c in range(chunks):
                mem_copy(m, c).wait_send()

        each(n_tm, lambda d: part_copy(m, d, tm).wait_send(), 1)
    each(n_tm, lambda d: q_copy(d, tm, tm).wait_send(), 1)

    def group_sent(d):
        cot_copy(d, me).wait_send()
        ctx_copy(d, me).wait_send()

    each(group, group_sent, 1)


def per_device(
    sizes,
    frames,
    block_mask,
    span_segment,
    dec_states,
    enc_qkv,
    enc_out,
    cross_query,
    cross_key,
    cross_value,
    cotangent,
):
    n_dp, n_sec, n_tm = sizes
    group = n_dp * n_tm
    qkv_full = lax.all_gather(enc_qkv[0], ("dp", "tm"), axis=0, tiled=True)
    out_full = lax.all_gather(enc_out[0], ("dp", "tm"), axis=1, tiled=True)
    cross_local = jnp.concatenate([cross_query, cross_key, cross_value], axis=1)
    cross_full = lax.all_gather(cross_local, ("dp", "tm"), axis=0, tiled=True)
    cross_width = cross_query.shape[1]
    query_full, both_full = cross_full[:, :cross_width], cross_full[:, cross_width:]
    tm = lax.axis_index("tm")
    rows, dim = frames.shape[1], frames.shape[2]
    width = out_full.shape[0]
    blocks = rows // BLK
    tokens = dec_states.shape[0] // MB

    index = tm * blocks + jnp.arange(blocks, dtype=jnp.int32)
    left_open = (block_mask[:, :, 0] == 1) & (index > 0)
    right_open = (block_mask[:, :, 1] == 1) & (index < blocks * n_tm - 1)
    window = jnp.arange(rows + 2 * BLK, dtype=jnp.int32) // BLK - 1
    own = jnp.arange(blocks, dtype=jnp.int32)
    offset = window[None, None, :] - own[None, :, None]
    seen = (
        (offset == 0)
        | ((offset == -1) & left_open[:, :, None])
        | ((offset == 1) & right_open[:, :, None])
    )
    enc_mask = jnp.repeat(seen.astype(jnp.float32), BLK, axis=1)
    segments = lax.dynamic_slice_in_dim(span_segment, tm * blocks, blocks, axis=1)
    frame_segment = jnp.repeat(segments, BLK, axis=1)
    token_segment = jnp.arange(n_tm * tokens, dtype=jnp.int32) // tokens
    cross_mask = (token_segment[None, :, None] == frame_segment[:, None, :]).astype(jnp.float32)
    cot = cotangent.reshape(MB * tokens, group, dim // group).transpose(1, 0, 2)

    bf, f32 = jnp.bfloat16, jnp.float32
    dma = pltpu.SemaphoreType.DMA
    vmem = pl.BlockSpec(memory_space=pltpu.VMEM)
    return pl.pallas_call(
        functools.partial(kernel, sizes),
        out_shape=(
            jax.ShapeDtypeStruct((MB * tokens, cross_width), bf),
            jax.ShapeDtypeStruct((cross_width, dim // group), f32),
        ),
        in_specs=[vmem] * 9,
        out_specs=(vmem, vmem),
        scratch_shapes=[
            pltpu.VMEM((MB, rows, dim), bf),
            pltpu.VMEM((MB, rows, dim), bf),
            pltpu.VMEM((MB, rows + 2 * BLK, 2 * width), bf),
            pltpu.VMEM((MB, rows, dim), bf),
            pltpu.VMEM((n_tm, MB, tokens, cross_width), bf),
            pltpu.VMEM((MB, n_tm, tokens, 2 * cross_width), f32),
            pltpu.VMEM((n_tm, MB, tokens, 2 * cross_width), f32),
            pltpu.VMEM((group, MB * tokens, cross_width), bf),
            pltpu.VMEM((group, MB * tokens, dim // group), bf),
            dma((MB,)),
            dma((MB,)),
            dma((2, MB)),
            dma((2, MB)),
            dma((MB, blocks)),
            dma((MB, blocks)),
            dma((n_tm,)),
            dma((n_tm,)),
            dma((MB, n_tm)),
            dma((MB, n_tm)),
            dma((group,)),
            dma((group,)),
            dma((group,)),
            dma((group,)),
        ],
        compiler_params=pltpu.CompilerParams(
            collective_id=0, has_side_effects=True, vmem_limit_bytes=56 * 2**20
        ),
    )(frames, enc_mask, cross_mask, dec_states, cot, qkv_full, out_full, query_full, both_full)


def solution(mesh):
    sizes = tuple(mesh.shape[a] for a in ("dp", "section", "tm"))
    in_specs = (
        P("dp", "tm", None),
        P("dp", "tm", None),
        P("dp", None),
        P(("dp", "tm"), None),
        P("section", ("dp", "tm"), None),
        P("section", None, ("dp", "tm")),
        P(("dp", "tm"), "section"),
        P(("dp", "tm"), "section"),
        P(("dp", "tm"), "section"),
        P(("dp", "tm"), None),
    )
    out_specs = (P(("dp", "tm"), "section"), P("section", ("dp", "tm")))
    return jax.shard_map(
        functools.partial(per_device, sizes),
        mesh=mesh,
        in_specs=in_specs,
        out_specs=out_specs,
        check_vma=False,
    )
```

profile of v0, /device:TPU:1, one launch (start us, length us, event | category | flops | bytes accessed | tf_op | source)
XLA Modules:
  0.0 204.4 jit_solution(5576595336014332615)
XLA Ops:
  7.2 0.0 all-gather.6.cloned.1.call-start
  7.2 1.8 pad_maximum_fusion
  9.0 0.0 all-gather.10.cloned.1.call-start
  9.1 0.7 all-gather.10.cloned.1.call-update
  9.8 0.0 all-gather.8.cloned.1.call-start
  9.8 0.7 all-gather.8.cloned.1.call-update
  10.5 0.1 constant_dynamic-slice_fusion
  10.6 0.1 broadcast_in_dim.5
  10.7 0.1 eq.65
  10.8 1.3 reshape.127
  12.0 0.8 copy.21
  12.8 0.2 and_reduce_fusion.1
  13.1 0.1 or_convert_fusion
  13.1 0.7 compare_convert_fusion.cross_mask
  13.9 24.5 %all-gather.6.cloned.1.call-done = bf16[1280,576]{1,0:T(8,128)(2,1)} async-done(((bf16[160,576]{1,0:T(8,128)(2,1)}), bf16[1280,576]{1,0:T(8,128)(2,1)}) %all-gather.6.cloned.1.call-update) | async-done | bytes 1474576 | tf_op jit(solution)/shard_map/all_gather | solution.py:337
  38.4 2.7 %slice.17.both_w = bf16[1280,384]{1,0:T(8,128)(2,1)} slice(bf16[1280,576]{1,0:T(8,128)(2,1)} %all-gather.6.cloned.1.call-done), slice={[0:1280], [192:576]} | slice | bytes 1966080 | tf_op jit(solution)/shard_map/slice | solution.py:339
  41.2 2.0 slice.16.query_w
  43.1 23.2 %all-gather.10.cloned.1.call-done = bf16[1,640,1280]{1,2,0:T(8,128)(2,1)} async-done(((bf16[1,640,160]{1,2,0:T(8,128)(2,1)}), bf16[1,640,1280]{1,2,0:T(8,128)(2,1)}) %all-gather.10.cloned.1.call-update) | async-done | bytes 1638416 | tf_op jit(solution)/shard_map/all_gather | solution.py:335
  66.3 3.5 %copy.18 = bf16[1,640,1280]{2,1,0:T(8,128)(2,1)} copy(bf16[1,640,1280]{1,2,0:T(8,128)(2,1)} %all-gather.10.cloned.1.call-done) | data formatting | bytes 3276800 | tf_op jit(solution)/shard_map/all_gather | solution.py:335
  69.9 38.1 %all-gather.8.cloned.1.call-done = bf16[1,1280,1920]{2,1,0:T(8,128)(2,1)} async-done(((bf16[1,160,1920]{2,1,0:T(8,128)(2,1)}), bf16[1,1280,1920]{2,1,0:T(8,128)(2,1)}) %all-gather.8.cloned.1.call-update) | async-done | bytes 4915216 | tf_op jit(solution)/shard_map/all_gather | solution.py:334
  108.0 0.7 broadcast_in_dim.4
  108.7 86.0 %shard_map.113 = (bf16[64,192]{1,0:T(8,128)(2,1)}, f32[192,160]{1,0:T(8,128)}) custom-call(bf16[2,128,1280]{2,1,0:T(8,128)(2,1)} %frames.1, f32[2,128,256]{2,1,0:T(8,128)} %bitcast.9, f32[2,128,128]{2,1,0:T(8,128)} %compare_convert_fusion.cross_mask, bf16[64,1280]{1,0:T(8,128)(2,1)} %dec.1, bf16[8,64,160]{2,1,0:T(8,128)(2,1)} %bitcast.8, ...), custom_call_target="tpu_custom_call" | custom-call | tf_op jit(solution)/shard_map/pallas_call | solution.py:367
  194.8 1.7 copy.19
  196.5 1.4 copy.23
  (9 shorter events, 0.1 us)
Async XLA Ops:
  7.2 3.4 %copy-start = (s32[2,8]{1,0:T(2,128)S(1)}, s32[2,8]{1,0:T(2,128)}, u32[]{:S(2)}) copy-start(s32[2,8]{1,0:T(2,128)} %param.12) | copy-start | bytes 196
  7.2 5.6 %copy-start.1 = (s32[2,2,2]{2,1,0:T(2,128)S(1)}, s32[2,2,2]{2,1,0:T(2,128)}, u32[]{:S(2)}) copy-start(s32[2,2,2]{2,1,0:T(2,128)} %param.11) | copy-start | bytes 100
  7.2 31.2 %all-gather.6.cloned.1.call-start = ((), (), s32[]{:S(2)}) async-start(), calls=%async_computation | async-start | bytes 1843200 | tf_op jit(solution)/shard_map/all_gather | solution.py:337
  9.0 57.3 %all-gather.10.cloned.1.call-start = ((), (), s32[]{:S(2)}) async-start(), calls=%async_computation.2 | async-start | bytes 1843200 | tf_op jit(solution)/shard_map/all_gather | solution.py:335
  9.8 98.2 %all-gather.8.cloned.1.call-start = ((), (), s32[]{:S(2)}) async-start(), calls=%async_computation.1 | async-start | bytes 5529600 | tf_op jit(solution)/shard_map/all_gather | solution.py:334
Sparse Core Ops, SparseCore 0:
  9.9 28.4 all-gather.5
  40.3 25.9 all-gather.9
  68.2 39.7 all-gather.7
where the time goes:
time: 205 us; the launch traced here: 204 us
  waiting for transfers between devices  87.2 us (43%)
  Pallas kernels  86 us (42%)
  local copies, waits for them, and re-layouts  14.3 us (7%)
  between operations  13.8 us (7%)
  other arithmetic  2.83 us (1%)
    pallas_call x1, Pallas kernels, per_device(): pl.pallas_call(functools.partial(kernel, sizes), out_shape=(jax.ShapeDtyp...  86 us
    all_gather x1, waiting for transfers between devices, per_device(): qkv_full = lax.all_gather(enc_qkv[0], ('dp', 'tm'), axis=0, tiled=True)  38.1 us
    all_gather x1, waiting for transfers between devices, per_device(): cross_full = lax.all_gather(cross_local, ('dp', 'tm'), axis=0, tiled=True)  24.5 us
    all_gather x1, waiting for transfers between devices, per_device(): out_full = lax.all_gather(enc_out[0], ('dp', 'tm'), axis=1, tiled=True)  23.2 us
  transfers between devices with their start and end apart: 3, of which 3 were waited for; matrix products, arithmetic and copies ran while one was open for 6% of the time, Pallas kernels for 0%

commit v1 on v0

--- a/solution.py
+++ b/solution.py
@@ -33,17 +33,22 @@
 
 def kernel(
     sizes,
+    spread,
     frames,
     enc_mask,
     cross_mask,
     dec,
     cot,
-    qkv,
-    out_w,
-    query_w,
-    both_w,
+    qkv_in,
+    out_in,
+    query_in,
+    key_in,
+    value_in,
     context_out,
     grad_out,
+    qkv,
+    out_t,
+    cross_w,
     xbuf,
     ybuf,
     kvbuf,
@@ -67,15 +72,17 @@
     ctx_recv,
     cot_send,
     cot_recv,
+    w_send,
+    w_recv,
 ):
     n_dp, n_sec, n_tm = sizes
     group = n_dp * n_tm
     dp, sec, tm = (lax.axis_index(a) for a in ("dp", "section", "tm"))
     me = dp * n_tm + tm
     rows = frames.shape[1]
-    width = out_w.shape[0]
+    width = out_t.shape[1]
     heads = width // HD
-    cross_width = query_w.shape[1]
+    cross_width = query_in.shape[1]
     cross_heads = cross_width // HD
     chunks = rows // BLK
     tokens = qall.shape[2]
@@ -133,6 +140,40 @@
         other, where = peer(d)
         return remote(cot.at[other], cot_all.at[slot], cot_send.at[d], cot_recv.at[slot], where)
 
+    weights_of = (qkv, out_t, cross_w)
+    share = qkv_in.shape[0]
+    half = share // 2
+    to_x = {"dp": 1 - dp}
+    to_y = {"tm": lax.rem(tm + 2, n_tm)}
+    to_core = {"tm": tm + 1 - 2 * lax.rem(tm, 2)}
+    from_x = (1 - dp) * n_tm + tm
+    from_y = dp * n_tm + lax.rem(tm + 2, n_tm)
+    from_both = (1 - dp) * n_tm + lax.rem(tm + 2, n_tm)
+    routes = [(me, 0, to_x), (me, 1, to_x), (me, 0, to_y), (me, 1, to_y), (from_x, 0, to_y), (from_y, 1, to_x)]
+    routes += [(o, h, to_core) for o in (me, from_x, from_y, from_both) for h in (0, 1)]
+
+    def w_copy(g, i):
+        owner, h, where = routes[i]
+        piece = weights_of[g].at[pl.ds(pl.multiple_of(owner * share + h * half, 16), half)]
+        return remote(piece, piece, w_send.at[g, i], w_recv.at[g, i], where)
+
+    def w_own(g):
+        for i in (0, 3, 1, 2, 6, 7):
+            w_copy(g, i).start()
+
+    def w_forward(g):
+        for got, passed in ((0, (4, 8)), (3, (5, 11))):
+            w_copy(g, got).wait_recv()
+            for i in passed:
+                w_copy(g, i).start()
+
+    def w_rest(g):
+        for got, passed in ((1, 9), (2, 10), (4, 12), (5, 13)):
+            w_copy(g, got).wait_recv()
+            w_copy(g, passed).start()
+        for i in range(6, 14):
+            w_copy(g, i).wait_recv()
+
     for m in range(MB):
         kvbuf[m, 0:BLK, :] = jnp.zeros((BLK, 2 * width), jnp.bfloat16)
         kvbuf[m, rows + BLK :, :] = jnp.zeros((BLK, 2 * width), jnp.bfloat16)
@@ -156,11 +197,31 @@
     near = jnp.where(sec > 0, 1, 0) + jnp.where(sec < n_sec - 1, 1, 0)
     pl.semaphore_wait(barrier, group - 1 + near)
 
+    base = pl.multiple_of(me * share, 16) if spread else 0
+    mine = pl.ds(base, share)
+    qkv[mine] = qkv_in[...]
+    if spread:
+        w_own(0)
+    out_t[mine] = out_in[...].T
+    cross_w[mine] = jnp.concatenate([key_in[...], value_in[...], query_in[...]], axis=1)
+    cot_all[me] = cot[me]
+    if spread:
+        w_forward(0)
+        w_own(1)
+        w_rest(0)
+        w_forward(1)
+        w_own(2)
+
+        @pl.when(sec > 0)
+        def _():
+            w_rest(1)
+            w_forward(2)
+            w_rest(2)
+
     each(group, lambda d: cot_copy(d, me).start(), 1)
-    cot_all[me] = cot[me]
 
     def queries():
-        values = dot_nn(norm_rows(dec[...]), query_w[...]).astype(jnp.bfloat16)
+        values = dot_nn(norm_rows(dec[...]), cross_w[:, 2 * cross_width :]).astype(jnp.bfloat16)
         qall[tm] = values.reshape(MB, tokens, cross_width)
         each(n_tm, lambda d: q_copy(d, tm, tm).start(), 1)
 
@@ -208,7 +269,12 @@
             value = kvbuf[m, :, width + h * HD : width + (h + 1) * HD]
             parts.append((dot_nn(weights.astype(jnp.bfloat16), value) / totals).astype(jnp.bfloat16))
         attended = jnp.concatenate(parts, axis=1)
-        update = dot_nn(attended, out_w[...])
+        if spread:
+            @pl.when(first & (m == 0))
+            def _():
+                w_rest(1)
+
+        update = dot_nt(attended, out_t[...])
         finished = (xbuf[m].astype(jnp.float32) + update).astype(jnp.bfloat16)
 
         @pl.when(sec < n_sec - 1)
@@ -227,6 +293,9 @@
 
     @pl.when(first)
     def _():
+        if spread:
+            w_forward(2)
+            w_rest(2)
         queries()
 
     def q_arrives(d):
@@ -245,7 +314,7 @@
             def _():
                 mem_copy(m, c).start()
 
-        key_value = dot_nn(memn[m], both_w[...]).astype(jnp.bfloat16)
+        key_value = dot_nn(memn[m], cross_w[:, : 2 * cross_width]).astype(jnp.bfloat16)
         query = qall[:, m].reshape(n_tm * tokens, cross_width)
         seen = cross_mask[m] > 0
         sums, denominators = [], []
@@ -309,6 +378,11 @@
         each(n_tm, lambda d: part_copy(m, d, tm).wait_send(), 1)
     each(n_tm, lambda d: q_copy(d, tm, tm).wait_send(), 1)
 
+    if spread:
+        for g in range(3):
+            for i in range(14):
+                w_copy(g, i).wait_send()
+
     def group_sent(d):
         cot_copy(d, me).wait_send()
         ctx_copy(d, me).wait_send()
@@ -331,15 +405,19 @@
 ):
     n_dp, n_sec, n_tm = sizes
     group = n_dp * n_tm
-    qkv_full = lax.all_gather(enc_qkv[0], ("dp", "tm"), axis=0, tiled=True)
-    out_full = lax.all_gather(enc_out[0], ("dp", "tm"), axis=1, tiled=True)
-    cross_local = jnp.concatenate([cross_query, cross_key, cross_value], axis=1)
-    cross_full = lax.all_gather(cross_local, ("dp", "tm"), axis=0, tiled=True)
+    qkv_w, out_w = enc_qkv[0], enc_out[0]
+    spread = n_dp == 2 and n_tm == 4 and qkv_w.shape[0] % 32 == 0 and out_w.shape[1] == qkv_w.shape[0]
+    if not spread:
+        qkv_w = lax.all_gather(qkv_w, ("dp", "tm"), axis=0, tiled=True)
+        out_w = lax.all_gather(out_w, ("dp", "tm"), axis=1, tiled=True)
+        cross_query, cross_key, cross_value = (
+            lax.all_gather(w, ("dp", "tm"), axis=0, tiled=True)
+            for w in (cross_query, cross_key, cross_value)
+        )
     cross_width = cross_query.shape[1]
-    query_full, both_full = cross_full[:, :cross_width], cross_full[:, cross_width:]
     tm = lax.axis_index("tm")
     rows, dim = frames.shape[1], frames.shape[2]
-    width = out_full.shape[0]
+    width = out_w.shape[0]
     blocks = rows // BLK
     tokens = dec_states.shape[0] // MB
 
@@ -365,14 +443,17 @@
     dma = pltpu.SemaphoreType.DMA
     vmem = pl.BlockSpec(memory_space=pltpu.VMEM)
     return pl.pallas_call(
-        functools.partial(kernel, sizes),
+        functools.partial(kernel, sizes, spread),
         out_shape=(
             jax.ShapeDtypeStruct((MB * tokens, cross_width), bf),
             jax.ShapeDtypeStruct((cross_width, dim // group), f32),
         ),
-        in_specs=[vmem] * 9,
+        in_specs=[vmem] * 10,
         out_specs=(vmem, vmem),
         scratch_shapes=[
+            pltpu.VMEM((dim, 3 * width), bf),
+            pltpu.VMEM((dim, width), bf),
+            pltpu.VMEM((dim, 3 * cross_width), bf),
             pltpu.VMEM((MB, rows, dim), bf),
             pltpu.VMEM((MB, rows, dim), bf),
             pltpu.VMEM((MB, rows + 2 * BLK, 2 * width), bf),
@@ -396,11 +477,13 @@
             dma((group,)),
             dma((group,)),
             dma((group,)),
+            dma((3, 14)),
+            dma((3, 14)),
         ],
         compiler_params=pltpu.CompilerParams(
             collective_id=0, has_side_effects=True, vmem_limit_bytes=56 * 2**20
         ),
-    )(frames, enc_mask, cross_mask, dec_states, cot, qkv_full, out_full, query_full, both_full)
+    )(frames, enc_mask, cross_mask, dec_states, cot, qkv_w, out_w, cross_query, cross_key, cross_value)
 
 
 def solution(mesh):

time: 205 us -> 131 us (0.64)
  waiting for transfers between devices: 87.2 us -> 0 us
  Pallas kernels: 86 us -> 122 us
  between operations: 13.8 us -> 0.69 us
  local copies, waits for them, and re-layouts: 14.3 us -> 7.12 us
    all_gather x3 -> x0, waiting for transfers between devices: 85.8 us -> none  [the longest x1 38.1 us: per_device(): qkv_full = lax.all_gather(enc_qkv[0], ('dp', 'tm'), axis=0, tiled=True)]
    pallas_call x1, Pallas kernels: 86 us -> 122 us  [per_device(): pl.pallas_call(functools.partial(kernel, sizes, spread), out_shape=(jax.S...]
    slice x2 -> x0, local copies, waits for them, and re-layouts: 4.71 us -> none  [the longest x1 2.74 us: per_device(): cross_full[:, cross_width:]]
    all_gather x1 -> x0, local copies, waits for them, and re-layouts: 3.54 us -> none  [per_device(): out_full = lax.all_gather(enc_out[0], ('dp', 'tm'), axis=1, tiled=True)]
  transfers between devices with their start and end apart: 3 -> 0, of which waited for: 3 -> 0; matrix products, arithmetic and copies ran while one was open for 6% -> 0% of each run, Pallas kernels for 0% -> 0%
where the time goes in v1:
time: 131 us
  Pallas kernels  122 us (93%)
  local copies, waits for them, and re-layouts  7.12 us (5%)
    pallas_call x1, Pallas kernels, per_device(): pl.pallas_call(functools.partial(kernel, sizes, spread), out_shape=(jax.S...  122 us
    unnamed x12, local copies, waits for them, and re-layouts  3.39 us

profile of v1, /device:TPU:1, one launch (start us, length us, event | category | flops | bytes accessed | tf_op | source)
XLA Modules:
  0.0 130.8 jit_solution(8163842149008906547)
XLA Ops:
  0.6 0.0 copy-start
  0.6 0.7 copy-done
  1.3 0.1 constant_dynamic-slice_fusion
  1.4 0.0 copy-start.4
  1.4 0.7 copy-done.4
  2.1 0.2 and_reduce_fusion.1
  2.3 0.1 broadcast_in_dim.5
  2.4 0.1 eq.65
  2.5 0.1 or_convert_fusion
  2.6 0.7 compare_convert_fusion.cross_mask
  3.3 0.0 copy-start.2
  3.3 0.7 broadcast_in_dim.4
  4.0 0.3 copy-done.2
  4.3 0.3 reshape.127
  4.7 0.0 copy-start.1
  4.7 0.7 copy.18
  5.4 0.2 copy-done.1
  5.6 0.9 copy.15
  6.5 121.9 %shard_map.113 = (bf16[64,192]{1,0:T(8,128)(2,1)}, f32[192,160]{1,0:T(8,128)}) custom-call(bf16[2,128,1280]{2,1,0:T(8,128)(2,1)} %frames.1, f32[2,128,256]{2,1,0:T(8,128)} %bitcast.7, f32[2,128,128]{2,1,0:T(8,128)} %compare_convert_fusion.cross_mask, bf16[64,1280]{1,0:T(8,128)(2,1)} %dec.1, bf16[8,64,160]{2,1,0:T(8,128)(2,1)} %bitcast.8, ...), custom_call_target="tpu_custom_call" | custom-call | tf_op jit(solution)/shard_map/pallas_call | solution.py:445
  128.5 0.0 copy-start.3
  128.5 1.7 %copy.16 = f32[192,160]{0,1:T(8,128)} copy(f32[192,160]{1,0:T(8,128)} %get-tuple-element.5) | data formatting | bytes 245760 | tf_op jit(solution)/shard_map/pallas_call | solution.py:445
  130.2 0.0 copy-done.3
  130.2 0.6 copy.20
  (4 shorter events, 0.0 us)
Async XLA Ops:
  0.6 0.7 copy-start
  1.4 0.7 copy-start.4
  3.3 1.0 copy-start.2
  4.7 1.0 copy-start.1
  128.5 1.7 %copy-start.3 = (bf16[64,192]{1,0:T(8,128)(2,1)S(1)}, bf16[64,192]{1,0:T(8,128)(2,1)}, u32[]{:S(2)}) copy-start(bf16[64,192]{1,0:T(8,128)(2,1)} %get-tuple-element.15) | copy-start | bytes 73732

commit v2 on v1

--- a/solution.py
+++ b/solution.py
@@ -10,6 +10,7 @@
 HD = 64
 BLK = 64
 MB = 2
+PIECE = 32
 
 MESH = pl.DeviceIdType.MESH
 epsilon = 1e-05
@@ -35,8 +36,8 @@
     sizes,
     spread,
     frames,
-    enc_mask,
-    cross_mask,
+    block_mask,
+    span,
     dec,
     cot,
     qkv_in,
@@ -49,6 +50,9 @@
     qkv,
     out_t,
     cross_w,
+    enc_mask,
+    cross_mask,
+    cot_split,
     xbuf,
     ybuf,
     kvbuf,
@@ -84,7 +88,7 @@
     heads = width // HD
     cross_width = query_in.shape[1]
     cross_heads = cross_width // HD
-    chunks = rows // BLK
+    chunks = rows // PIECE
     tokens = qall.shape[2]
     first, last = sec == 0, sec == n_sec - 1
 
@@ -117,7 +121,7 @@
 
     def mem_copy(m, c):
         return remote(
-            memn.at[m, pl.ds(c * BLK, BLK)], memn.at[m, pl.ds(c * BLK, BLK)],
+            memn.at[m, pl.ds(c * PIECE, PIECE)], memn.at[m, pl.ds(c * PIECE, PIECE)],
             mem_send.at[m, c], mem_recv.at[m, c], {"section": sec - 1},
         )
 
@@ -138,7 +142,7 @@
 
     def cot_copy(d, slot):
         other, where = peer(d)
-        return remote(cot.at[other], cot_all.at[slot], cot_send.at[d], cot_recv.at[slot], where)
+        return remote(cot_split.at[other], cot_all.at[slot], cot_send.at[d], cot_recv.at[slot], where)
 
     weights_of = (qkv, out_t, cross_w)
     share = qkv_in.shape[0]
@@ -197,14 +201,42 @@
     near = jnp.where(sec > 0, 1, 0) + jnp.where(sec < n_sec - 1, 1, 0)
     pl.semaphore_wait(barrier, group - 1 + near)
 
+    share_cols = cot_split.shape[2]
+
+    def make_masks():
+        blocks = rows // BLK
+        column = lax.broadcasted_iota(jnp.int32, (BLK, rows + 2 * BLK), 1) // BLK
+        frame_block = lax.broadcasted_iota(jnp.int32, (1, rows), 1) // BLK
+        row_segment = lax.broadcasted_iota(jnp.int32, (n_tm * tokens, rows), 0) // tokens
+        for m in range(MB):
+            served = jnp.zeros((1, rows), jnp.int32)
+            segments = span[m : m + 1, :]
+            place = lax.broadcasted_iota(jnp.int32, segments.shape, 1)
+            for b in range(blocks):
+                index = tm * blocks + b
+                before = jnp.where(index > 0, block_mask[m, b : b + 1, 0:1], 0)
+                after = jnp.where(index < n_tm * blocks - 1, block_mask[m, b : b + 1, 1:2], 0)
+                seen = jnp.where(column == b + 1, 1, 0)
+                seen = jnp.where(column == b, before, seen)
+                seen = jnp.where(column == b + 2, after, seen)
+                enc_mask[m, b * BLK : (b + 1) * BLK, :] = seen.astype(jnp.float32)
+                one = jnp.sum(
+                    jnp.where(place == index, segments, 0).astype(jnp.float32), axis=1, keepdims=True
+                ).astype(jnp.int32)
+                served = jnp.where(frame_block == b, one, served)
+            cross_mask[m] = jnp.where(row_segment == served, 1.0, 0.0)
+
     base = pl.multiple_of(me * share, 16) if spread else 0
     mine = pl.ds(base, share)
     qkv[mine] = qkv_in[...]
     if spread:
         w_own(0)
-    out_t[mine] = out_in[...].T
+    out_t[mine] = out_in[...]
     cross_w[mine] = jnp.concatenate([key_in[...], value_in[...], query_in[...]], axis=1)
-    cot_all[me] = cot[me]
+    for i in range(group):
+        cot_split[i] = cot[:, i * share_cols : (i + 1) * share_cols]
+    cot_all[me] = cot_split[me]
+    make_masks()
     if spread:
         w_forward(0)
         w_own(1)
@@ -352,9 +384,9 @@
 
     each(group, arrivals, 1)
     left = ctx_all[...].reshape(group * MB * tokens, cross_width)
-    right = cot_all[...].reshape(group * MB * tokens, cot.shape[2])
+    right = cot_all[...].reshape(group * MB * tokens, cot_split.shape[2])
     grad_out[...] = lax.dot_general(
-        left, right, (((0,), (0,)), ((), ())), preferred_element_type=jnp.float32
+        right, left, (((0,), (0,)), ((), ())), preferred_element_type=jnp.float32
     )
 
     for m in range(MB):
@@ -405,48 +437,28 @@
 ):
     n_dp, n_sec, n_tm = sizes
     group = n_dp * n_tm
-    qkv_w, out_w = enc_qkv[0], enc_out[0]
-    spread = n_dp == 2 and n_tm == 4 and qkv_w.shape[0] % 32 == 0 and out_w.shape[1] == qkv_w.shape[0]
+    qkv_w, out_w = enc_qkv[0], enc_out[0].T
+    spread = n_dp == 2 and n_tm == 4 and qkv_w.shape[0] % 32 == 0 and out_w.shape[0] == qkv_w.shape[0]
     if not spread:
         qkv_w = lax.all_gather(qkv_w, ("dp", "tm"), axis=0, tiled=True)
-        out_w = lax.all_gather(out_w, ("dp", "tm"), axis=1, tiled=True)
+        out_w = lax.all_gather(out_w, ("dp", "tm"), axis=0, tiled=True)
         cross_query, cross_key, cross_value = (
             lax.all_gather(w, ("dp", "tm"), axis=0, tiled=True)
             for w in (cross_query, cross_key, cross_value)
         )
     cross_width = cross_query.shape[1]
-    tm = lax.axis_index("tm")
     rows, dim = frames.shape[1], frames.shape[2]
-    width = out_w.shape[0]
-    blocks = rows // BLK
+    width = out_w.shape[1]
     tokens = dec_states.shape[0] // MB
-
-    index = tm * blocks + jnp.arange(blocks, dtype=jnp.int32)
-    left_open = (block_mask[:, :, 0] == 1) & (index > 0)
-    right_open = (block_mask[:, :, 1] == 1) & (index < blocks * n_tm - 1)
-    window = jnp.arange(rows + 2 * BLK, dtype=jnp.int32) // BLK - 1
-    own = jnp.arange(blocks, dtype=jnp.int32)
-    offset = window[None, None, :] - own[None, :, None]
-    seen = (
-        (offset == 0)
-        | ((offset == -1) & left_open[:, :, None])
-        | ((offset == 1) & right_open[:, :, None])
-    )
-    enc_mask = jnp.repeat(seen.astype(jnp.float32), BLK, axis=1)
-    segments = lax.dynamic_slice_in_dim(span_segment, tm * blocks, blocks, axis=1)
-    frame_segment = jnp.repeat(segments, BLK, axis=1)
-    token_segment = jnp.arange(n_tm * tokens, dtype=jnp.int32) // tokens
-    cross_mask = (token_segment[None, :, None] == frame_segment[:, None, :]).astype(jnp.float32)
-    cot = cotangent.reshape(MB * tokens, group, dim // group).transpose(1, 0, 2)
 
     bf, f32 = jnp.bfloat16, jnp.float32
     dma = pltpu.SemaphoreType.DMA
     vmem = pl.BlockSpec(memory_space=pltpu.VMEM)
-    return pl.pallas_call(
+    context, grad_t = pl.pallas_call(
         functools.partial(kernel, sizes, spread),
         out_shape=(
             jax.ShapeDtypeStruct((MB * tokens, cross_width), bf),
-            jax.ShapeDtypeStruct((cross_width, dim // group), f32),
+            jax.ShapeDtypeStruct((dim // group, cross_width), f32),
         ),
         in_specs=[vmem] * 10,
         out_specs=(vmem, vmem),
@@ -454,6 +466,9 @@
             pltpu.VMEM((dim, 3 * width), bf),
             pltpu.VMEM((dim, width), bf),
             pltpu.VMEM((dim, 3 * cross_width), bf),
+            pltpu.VMEM((MB, rows, rows + 2 * BLK), f32),
+            pltpu.VMEM((MB, n_tm * tokens, rows), f32),
+            pltpu.VMEM((group, MB * tokens, dim // group), bf),
             pltpu.VMEM((MB, rows, dim), bf),
             pltpu.VMEM((MB, rows, dim), bf),
             pltpu.VMEM((MB, rows + 2 * BLK, 2 * width), bf),
@@ -467,8 +482,8 @@
             dma((MB,)),
             dma((2, MB)),
             dma((2, MB)),
-            dma((MB, blocks)),
-            dma((MB, blocks)),
+            dma((MB, rows // PIECE)),
+            dma((MB, rows // PIECE)),
             dma((n_tm,)),
             dma((n_tm,)),
             dma((MB, n_tm)),
@@ -483,7 +498,8 @@
         compiler_params=pltpu.CompilerParams(
             collective_id=0, has_side_effects=True, vmem_limit_bytes=56 * 2**20
         ),
-    )(frames, enc_mask, cross_mask, dec_states, cot, qkv_w, out_w, cross_query, cross_key, cross_value)
+    )(frames, block_mask, span_segment, dec_states, cotangent, qkv_w, out_w, cross_query, cross_key, cross_value)
+    return context, grad_t.T
 
 
 def solution(mesh):

time: 131 us -> 122 us (0.931)
  local copies, waits for them, and re-layouts: 7.12 us -> 2.97 us
  Pallas kernels: 122 us -> 119 us
    pallas_call x1, Pallas kernels: 122 us -> 119 us  [per_device(): pl.pallas_call(functools.partial(kernel, sizes, spread), out_shape=(jax.S...]
    pallas_call x1 -> x0, local copies, waits for them, and re-layouts: 1.71 us -> none  [per_device(): pl.pallas_call(functools.partial(kernel, sizes, spread), out_shape=(jax.S...]
    unnamed x12 -> x2, local copies, waits for them, and re-layouts: 3.39 us -> 2.97 us
where the time goes in v2:
time: 122 us
  Pallas kernels  119 us (98%)
  local copies, waits for them, and re-layouts  2.97 us (2%)
    pallas_call x1, Pallas kernels, per_device(): pl.pallas_call(functools.partial(kernel, sizes, spread), out_shape=(jax.S...  119 us
    unnamed x2, local copies, waits for them, and re-layouts  2.97 us

profile of v2, /device:TPU:1, one launch (start us, length us, event | category | flops | bytes accessed | tf_op | source)
XLA Modules:
  0.0 122.2 jit_solution(7084340924220397773)
XLA Ops:
  0.6 118.6 %shard_map.113 = (bf16[64,192]{1,0:T(8,128)(2,1)}, f32[160,192]{1,0:T(8,128)}) custom-call(bf16[2,128,1280]{2,1,0:T(8,128)(2,1)} %frames.1, s32[2,2,2]{2,1,0:T(2,128)} %block_mask.1, s32[2,8]{1,0:T(2,128)} %span.1, bf16[64,1280]{1,0:T(8,128)(2,1)} %dec.1, bf16[64,1280]{1,0:T(8,128)(2,1)} %cot.1, bf16[160,1920]{1,0:T(8,128)(2,1)} %bitcast.5, ...), custom_call_target="tpu_custom_call" | custom-call | tf_op jit(solution)/shard_map/pallas_call | solution.py:457
  119.2 1.4 %copy.14 = bf16[64,192]{1,0:T(8,128)(2,1)} copy(bf16[64,192]{1,0:T(8,128)(2,1)} %get-tuple-element.8) | data formatting | bytes 49152
  120.6 1.6 %copy.15 = f32[192,160]{0,1:T(8,128)} copy(f32[192,160]{0,1:T(8,128)} %bitcast.7) | data formatting | bytes 245760

commit v3 on v2

--- a/solution.py
+++ b/solution.py
@@ -104,8 +104,11 @@
     def each(count, body, start=0):
         lax.fori_loop(start, count, lambda i, c: (body(i), c)[1], 0)
 
-    def x_copy(m):
-        return remote(ybuf.at[m], xbuf.at[m], x_send.at[m], x_recv.at[m], {"section": sec + 1})
+    def x_copy(m, b):
+        block = pl.ds(b * BLK, BLK)
+        return remote(
+            ybuf.at[m, block], xbuf.at[m, block], x_send.at[m, b], x_recv.at[m, b], {"section": sec + 1}
+        )
 
     def halo_up(m):
         return remote(
@@ -205,7 +208,7 @@
 
     def make_masks():
         blocks = rows // BLK
-        column = lax.broadcasted_iota(jnp.int32, (BLK, rows + 2 * BLK), 1) // BLK
+        column = lax.broadcasted_iota(jnp.int32, (BLK, 3 * BLK), 1) // BLK
         frame_block = lax.broadcasted_iota(jnp.int32, (1, rows), 1) // BLK
         row_segment = lax.broadcasted_iota(jnp.int32, (n_tm * tokens, rows), 0) // tokens
         for m in range(MB):
@@ -216,9 +219,7 @@
                 index = tm * blocks + b
                 before = jnp.where(index > 0, block_mask[m, b : b + 1, 0:1], 0)
                 after = jnp.where(index < n_tm * blocks - 1, block_mask[m, b : b + 1, 1:2], 0)
-                seen = jnp.where(column == b + 1, 1, 0)
-                seen = jnp.where(column == b, before, seen)
-                seen = jnp.where(column == b + 2, after, seen)
+                seen = jnp.where(column == 0, before, jnp.where(column == 2, after, 1))
                 enc_mask[m, b * BLK : (b + 1) * BLK, :] = seen.astype(jnp.float32)
                 one = jnp.sum(
                     jnp.where(place == index, segments, 0).astype(jnp.float32), axis=1, keepdims=True
@@ -266,11 +267,14 @@
         def _():
             xbuf[m] = frames[m]
 
-        @pl.when(sec > 0)
-        def _():
-            x_copy(m).wait_recv()
-
-        normed = norm_rows(xbuf[m])
+        pieces = []
+        for b in range(rows // BLK):
+            @pl.when(sec > 0)
+            def _():
+                x_copy(m, b).wait_recv()
+
+            pieces.append(norm_rows(xbuf[m, b * BLK : (b + 1) * BLK, :]))
+        normed = jnp.concatenate(pieces, axis=0)
         kvbuf[m, BLK : BLK + rows, :] = dot_nn(normed, qkv[:, width:]).astype(jnp.bfloat16)
 
         @pl.when(tm < n_tm - 1)
@@ -283,43 +287,48 @@
 
         query = dot_nn(normed, qkv[:, :width]).astype(jnp.bfloat16)
 
-        @pl.when(tm > 0)
-        def _():
-            halo_up(m).wait_recv()
-
-        @pl.when(tm < n_tm - 1)
-        def _():
-            halo_down(m).wait_recv()
-
-        seen = enc_mask[m] > 0
-        parts = []
-        for h in range(heads):
-            cols = slice(h * HD, (h + 1) * HD)
-            scores = dot_nt(query[:, cols], kvbuf[m, :, cols]) * SCALE
-            weights = jnp.where(seen, jnp.exp(scores), 0.0)
-            totals = jnp.sum(weights, axis=-1, keepdims=True)
-            value = kvbuf[m, :, width + h * HD : width + (h + 1) * HD]
-            parts.append((dot_nn(weights.astype(jnp.bfloat16), value) / totals).astype(jnp.bfloat16))
-        attended = jnp.concatenate(parts, axis=1)
-        if spread:
-            @pl.when(first & (m == 0))
+        for b in range(rows // BLK):
+            if b == 0:
+                @pl.when(tm > 0)
+                def _():
+                    halo_up(m).wait_recv()
+
+            if b == rows // BLK - 1:
+                @pl.when(tm < n_tm - 1)
+                def _():
+                    halo_down(m).wait_recv()
+
+            block = slice(b * BLK, (b + 1) * BLK)
+            around = slice(b * BLK, (b + 3) * BLK)
+            seen = enc_mask[m, block, :] > 0
+            parts = []
+            for h in range(heads):
+                cols = slice(h * HD, (h + 1) * HD)
+                scores = dot_nt(query[block, cols], kvbuf[m, around, cols]) * SCALE
+                weights = jnp.where(seen, jnp.exp(scores), 0.0)
+                totals = jnp.sum(weights, axis=-1, keepdims=True)
+                value = kvbuf[m, around, width + h * HD : width + (h + 1) * HD]
+                parts.append((dot_nn(weights.astype(jnp.bfloat16), value) / totals).astype(jnp.bfloat16))
+            attended = jnp.concatenate(parts, axis=1)
+            if spread and b == 0:
+                @pl.when(first & (m == 0))
+                def _():
+                    w_rest(1)
+
+            update = dot_nt(attended, out_t[...])
+            finished = (xbuf[m, block, :].astype(jnp.float32) + update).astype(jnp.bfloat16)
+
+            @pl.when(sec < n_sec - 1)
             def _():
-                w_rest(1)
-
-        update = dot_nt(attended, out_t[...])
-        finished = (xbuf[m].astype(jnp.float32) + update).astype(jnp.bfloat16)
-
-        @pl.when(sec < n_sec - 1)
-        def _():
-            ybuf[m] = finished
-            x_copy(m).start()
-
-        @pl.when(last)
-        def _():
-            memn[m] = norm_rows(finished)
-            if n_sec > 1:
-                for c in range(chunks):
-                    mem_copy(m, c).start()
+                ybuf[m, block, :] = finished
+                x_copy(m, b).start()
+
+            @pl.when(last)
+            def _():
+                memn[m, block, :] = norm_rows(finished)
+                if n_sec > 1:
+                    for c in range(b * BLK // PIECE, (b + 1) * BLK // PIECE):
+                        mem_copy(m, c).start()
 
     each(MB, encode)
 
@@ -392,7 +401,8 @@
     for m in range(MB):
         @pl.when(sec < n_sec - 1)
         def _():
-            x_copy(m).wait_send()
+            for b in range(rows // BLK):
+                x_copy(m, b).wait_send()
 
         @pl.when(tm < n_tm - 1)
         def _():
@@ -466,7 +476,7 @@
             pltpu.VMEM((dim, 3 * width), bf),
             pltpu.VMEM((dim, width), bf),
             pltpu.VMEM((dim, 3 * cross_width), bf),
-            pltpu.VMEM((MB, rows, rows + 2 * BLK), f32),
+            pltpu.VMEM((MB, rows, 3 * BLK), f32),
             pltpu.VMEM((MB, n_tm * tokens, rows), f32),
             pltpu.VMEM((group, MB * tokens, dim // group), bf),
             pltpu.VMEM((MB, rows, dim), bf),
@@ -478,8 +488,8 @@
             pltpu.VMEM((n_tm, MB, tokens, 2 * cross_width), f32),
             pltpu.VMEM((group, MB * tokens, cross_width), bf),
             pltpu.VMEM((group, MB * tokens, dim // group), bf),
-            dma((MB,)),
-            dma((MB,)),
+            dma((MB, rows // BLK)),
+            dma((MB, rows // BLK)),
             dma((2, MB)),
             dma((2, MB)),
             dma((MB, rows // PIECE)),

time: 122 us -> 127 us (1.041)
  Pallas kernels: 119 us -> 123 us
    pallas_call x1, Pallas kernels: 119 us -> 123 us  [per_device(): pl.pallas_call(functools.partial(kernel, sizes, spread), out_shape=(jax.S...]
where the time goes in v3:
time: 127 us
  Pallas kernels  123 us (97%)
  local copies, waits for them, and re-layouts  2.97 us (2%)
    pallas_call x1, Pallas kernels, per_device(): pl.pallas_call(functools.partial(kernel, sizes, spread), out_shape=(jax.S...  123 us
    unnamed x2, local copies, waits for them, and re-layouts  2.97 us

profile of v3, /device:TPU:1, one launch (start us, length us, event | category | flops | bytes accessed | tf_op | source)
XLA Modules:
  0.0 126.5 jit_solution(7622795085347672975)
XLA Ops:
  0.6 122.9 %shard_map.113 = (bf16[64,192]{1,0:T(8,128)(2,1)}, f32[160,192]{1,0:T(8,128)}) custom-call(bf16[2,128,1280]{2,1,0:T(8,128)(2,1)} %frames.1, s32[2,2,2]{2,1,0:T(2,128)} %block_mask.1, s32[2,8]{1,0:T(2,128)} %span.1, bf16[64,1280]{1,0:T(8,128)(2,1)} %dec.1, bf16[64,1280]{1,0:T(8,128)(2,1)} %cot.1, bf16[160,1920]{1,0:T(8,128)(2,1)} %bitcast.5, ...), custom_call_target="tpu_custom_call" | custom-call | tf_op jit(solution)/shard_map/pallas_call | solution.py:467
  123.6 1.4 %copy.14 = bf16[64,192]{1,0:T(8,128)(2,1)} copy(bf16[64,192]{1,0:T(8,128)(2,1)} %get-tuple-element.8) | data formatting | bytes 49152
  124.9 1.6 %copy.15 = f32[192,160]{0,1:T(8,128)} copy(f32[192,160]{0,1:T(8,128)} %bitcast.7) | data formatting | bytes 245760

commit v4 on v2

--- a/solution.py
+++ b/solution.py
@@ -281,7 +281,8 @@
         def _():
             halo_down(m).start()
 
-        query = dot_nn(normed, qkv[:, :width]).astype(jnp.bfloat16)
+        query = dot_nn(normed, qkv[:, :width]) * SCALE
+        low = lax.broadcasted_iota(jnp.int32, (rows, 2 * HD), 1) < HD
 
         @pl.when(tm > 0)
         def _():
@@ -291,15 +292,20 @@
         def _():
             halo_down(m).wait_recv()
 
-        seen = enc_mask[m] > 0
+        seen = jnp.concatenate([enc_mask[m], enc_mask[m]], axis=0) > 0
         parts = []
-        for h in range(heads):
-            cols = slice(h * HD, (h + 1) * HD)
-            scores = dot_nt(query[:, cols], kvbuf[m, :, cols]) * SCALE
-            weights = jnp.where(seen, jnp.exp(scores), 0.0)
+        for pair in range(heads // 2):
+            cols = slice(pair * 2 * HD, (pair + 1) * 2 * HD)
+            mixed = query[:, cols]
+            stacked = jnp.concatenate(
+                [jnp.where(low, mixed, 0.0), jnp.where(low, 0.0, mixed)], axis=0
+            ).astype(jnp.bfloat16)
+            weights = jnp.where(seen, jnp.exp(dot_nt(stacked, kvbuf[m, :, cols])), 0.0)
             totals = jnp.sum(weights, axis=-1, keepdims=True)
-            value = kvbuf[m, :, width + h * HD : width + (h + 1) * HD]
-            parts.append((dot_nn(weights.astype(jnp.bfloat16), value) / totals).astype(jnp.bfloat16))
+            value = kvbuf[m, :, width + pair * 2 * HD : width + (pair + 1) * 2 * HD]
+            summed = dot_nn(weights.astype(jnp.bfloat16), value)
+            top = jnp.where(low, summed[:rows], summed[rows:])
+            parts.append((top / jnp.where(low, totals[:rows], totals[rows:])).astype(jnp.bfloat16))
         attended = jnp.concatenate(parts, axis=1)
         if spread:
             @pl.when(first & (m == 0))

time: 122 us -> 123 us (level)
  no operation moved by 1% of the time
where the time goes in v4:
time: 123 us; the launch traced here: 122 us
  Pallas kernels  119 us (97%)
  local copies, waits for them, and re-layouts  2.97 us (2%)
    pallas_call x1, Pallas kernels, per_device(): pl.pallas_call(functools.partial(kernel, sizes, spread), out_shape=(jax.S...  119 us
    unnamed x2, local copies, waits for them, and re-layouts  2.97 us

profile of v4, /device:TPU:1, one launch (start us, length us, event | category | flops | bytes accessed | tf_op | source)
XLA Modules:
  0.0 122.4 jit_solution(9910072150603439800)
XLA Ops:
  0.6 118.8 %shard_map.113 = (bf16[64,192]{1,0:T(8,128)(2,1)}, f32[160,192]{1,0:T(8,128)}) custom-call(bf16[2,128,1280]{2,1,0:T(8,128)(2,1)} %frames.1, s32[2,2,2]{2,1,0:T(2,128)} %block_mask.1, s32[2,8]{1,0:T(2,128)} %span.1, bf16[64,1280]{1,0:T(8,128)(2,1)} %dec.1, bf16[64,1280]{1,0:T(8,128)(2,1)} %cot.1, bf16[160,1920]{1,0:T(8,128)(2,1)} %bitcast.5, ...), custom_call_target="tpu_custom_call" | custom-call | tf_op jit(solution)/shard_map/pallas_call | solution.py:463
  119.4 1.4 %copy.14 = bf16[64,192]{1,0:T(8,128)(2,1)} copy(bf16[64,192]{1,0:T(8,128)(2,1)} %get-tuple-element.8) | data formatting | bytes 49152
  120.8 1.6 %copy.15 = f32[192,160]{0,1:T(8,128)} copy(f32[192,160]{0,1:T(8,128)} %bitcast.7) | data formatting | bytes 245760

commit v5 on v2

--- a/solution.py
+++ b/solution.py
@@ -171,6 +171,9 @@
             for i in passed:
                 w_copy(g, i).start()
 
+    def cot_sends():
+        each(group, lambda d: cot_copy(d, me).start(), 1)
+
     def w_rest(g):
         for got, passed in ((1, 9), (2, 10), (4, 12), (5, 13)):
             w_copy(g, got).wait_recv()
@@ -242,15 +245,17 @@
         w_own(1)
         w_rest(0)
         w_forward(1)
-        w_own(2)
 
         @pl.when(sec > 0)
         def _():
+            w_own(2)
+            cot_sends()
             w_rest(1)
             w_forward(2)
             w_rest(2)
 
-    each(group, lambda d: cot_copy(d, me).start(), 1)
+    if not spread:
+        cot_sends()
 
     def queries():
         values = dot_nn(norm_rows(dec[...]), cross_w[:, 2 * cross_width :]).astype(jnp.bfloat16)
@@ -305,6 +310,8 @@
             @pl.when(first & (m == 0))
             def _():
                 w_rest(1)
+                w_own(2)
+                cot_sends()
 
         update = dot_nt(attended, out_t[...])
         finished = (xbuf[m].astype(jnp.float32) + update).astype(jnp.bfloat16)

time: 122 us -> 116 us (0.951)
  Pallas kernels: 119 us -> 112 us
    pallas_call x1, Pallas kernels: 119 us -> 112 us  [per_device(): pl.pallas_call(functools.partial(kernel, sizes, spread), out_shape=(jax.S...]
where the time goes in v5:
time: 116 us
  Pallas kernels  112 us (97%)
  local copies, waits for them, and re-layouts  2.97 us (3%)
    pallas_call x1, Pallas kernels, per_device(): pl.pallas_call(functools.partial(kernel, sizes, spread), out_shape=(jax.S...  112 us
    unnamed x2, local copies, waits for them, and re-layouts  2.97 us

profile of v5, /device:TPU:1, one launch (start us, length us, event | category | flops | bytes accessed | tf_op | source)
XLA Modules:
  0.0 115.9 jit_solution(14209577456693743200)
XLA Ops:
  0.6 112.3 %shard_map.113 = (bf16[64,192]{1,0:T(8,128)(2,1)}, f32[160,192]{1,0:T(8,128)}) custom-call(bf16[2,128,1280]{2,1,0:T(8,128)(2,1)} %frames.1, s32[2,2,2]{2,1,0:T(2,128)} %block_mask.1, s32[2,8]{1,0:T(2,128)} %span.1, bf16[64,1280]{1,0:T(8,128)(2,1)} %dec.1, bf16[64,1280]{1,0:T(8,128)(2,1)} %cot.1, bf16[160,1920]{1,0:T(8,128)(2,1)} %bitcast.5, ...), custom_call_target="tpu_custom_call" | custom-call | tf_op jit(solution)/shard_map/pallas_call | solution.py:464
  112.9 1.4 %copy.14 = bf16[64,192]{1,0:T(8,128)(2,1)} copy(bf16[64,192]{1,0:T(8,128)(2,1)} %get-tuple-element.8) | data formatting | bytes 49152
  114.3 1.6 %copy.15 = f32[192,160]{0,1:T(8,128)} copy(f32[192,160]{0,1:T(8,128)} %bitcast.7) | data formatting | bytes 245760
